TPU v7x, 256 devices: a whole 4x4x8 slice. The times are simulated.
256 devices in a mesh: gx: 16 (over y, x_lo, core), gy: 16 (over z, x_hi).
Axes of the slice: x: 4 (x_hi: 2, x_lo: 2; x = x_hi * 2 + x_lo), y: 4, z: 8, core: 2. Of those that a mesh axis runs over, the one named last changes fastest.
Arguments:
- features: bfloat16 [65536, 128], P(('gx', 'gy')), may hold values from -6 to 6
- w_sub: bfloat16 [27, 128, 128], replicated, may hold values from -0.1875 to 0.1875
- w_down: bfloat16 [1024, 256], replicated, may hold values from -0.25 to 0.25
- cell_ids: int32 [65536], P(('gx', 'gy')), may hold values from -1 to 511, as said below
- send_rows: int32 [73728], P(('gx', 'gy')), may hold values from 0 to 256, as said below
- map_in: int32 [27, 65536], P(None, ('gx', 'gy')), may hold values from 0 to 608, as said below
- map_out: int32 [27, 65536], P(None, ('gx', 'gy')), may hold values from 0 to 256, as said below
- cotangent: bfloat16 [16384, 256], P(('gx', 'gy')), may hold values from -6 to 6
Outputs:
- coarse: bfloat16 [16384, 256], P(('gx', 'gy'))
- feature_grad: bfloat16 [65536, 128], P(('gx', 'gy'))
- sub_grad: float32 [27, 128, 128], replicated
- down_grad: float32 [1024, 256], replicated
Inputs may be any that keep to these rules, and one draw needn't show every extreme that they name: `cell_ids`: in every region the used rows are 0 to count - 1, in increasing cell number; -1 marks unused rows; a region uses at most 256 rows and some region uses exactly 256. `send_rows`: the row of the voxel at each rim cell, 256 where the cell is empty; rim cells listed in increasing cell number. `map_in`: indices into lookup_table: below 256 own rows, 257 + g ghost row g; within each offset the pairs come in increasing output row, and unused entries stand at the end with the value 256. A pair exists exactly where the output voxel and the voxel at its offset both exist. `map_out`: the output row of each pair; 256 on unused entries at the end of each offset's list; each row appears at most once per offset.
All inputs are finite; a program needn't handle non-finite values.
Results may differ from a plain program's by a relative error of at most 0.015.
Values may be sent and summed in bfloat16 or wider, within the bound.
No kernel may reach another device: no remote copies, remote signals or barrier semaphores. Data moves between devices by JAX's collectives and lax.ppermute only.
A program may use at most 64 MiB of HBM per device.

v0:
```python
import jax
import jax.numpy as jnp
import numpy as np
from jax import lax
from jax.sharding import PartitionSpec as P

LX = 4
LY = 16
LZ = 8
U_DEV = 64


def shifted(value, axis, by):
    peers = lax.axis_size(axis)
    pairs = [(i, i + by) for i in range(peers) if 0 <= i + by < peers]
    return lax.ppermute(value, axis, pairs)


def with_halo(block, sides, width):
    for axis, dim in sides:
        count = lax.axis_size(axis)
        forward = [(i, i + 1) for i in range(count - 1)]
        backward = [(target, source) for source, target in forward]
        low = lax.ppermute(
            lax.slice_in_dim(block, block.shape[dim] - width, None, axis=dim), axis, forward
        )
        high = lax.ppermute(lax.slice_in_dim(block, 0, width, axis=dim), axis, backward)
        block = jnp.concatenate([low, block, high], axis=dim)
    return block


def frame_tables():
    cell_count = LX * LY * LZ
    cell_index = np.arange(cell_count)
    coord_x = cell_index // (LY * LZ)
    coord_y = cell_index // LZ % LY
    on_rim = (coord_x == 0) | (coord_x == LX - 1) | (coord_y == 0) | (coord_y == LY - 1)
    rim_place = np.full(cell_count, -1, np.int64)
    rim_place[on_rim] = np.arange(int(on_rim.sum()))
    depth_range = np.arange(LZ)
    neighbour_list, face_list, side_list = ([], [], [])
    for frame_x in range(-1, LX + 1):
        for frame_y in range(-1, LY + 1):
            if 0 <= frame_x < LX and 0 <= frame_y < LY:
                continue
            step_x = -1 if frame_x < 0 else 1 if frame_x >= LX else 0
            step_y = -1 if frame_y < 0 else 1 if frame_y >= LY else 0
            local_cell = ((frame_x - step_x * LX) * LY + (frame_y - step_y * LY)) * LZ + depth_range
            neighbour_list.append(np.full(LZ, (step_x + 1) * 3 + step_y + 1))
            face_list.append(rim_place[local_cell])
            if 0 <= frame_y < LY:
                first_place = (0 if frame_x < 0 else LY * LZ) + frame_y * LZ
            else:
                column = frame_x if 0 <= frame_x < LX else LX if frame_x < 0 else LX + 1
                first_place = 2 * LY * LZ + (0 if frame_y < 0 else (LX + 2) * LZ) + column * LZ
            side_list.append(first_place + depth_range)
    side_place = np.concatenate(side_list)

    def face_rows(spots):
        return np.concatenate(
            [rim_place[(spot_x * LY + spot_y) * LZ + depth_range] for spot_x, spot_y in spots]
        )

    return {
        "neighbour": np.concatenate(neighbour_list),
        "face": np.concatenate(face_list),
        "side_place": side_place,
        "side_order": np.argsort(side_place),
        "x_high": face_rows([(LX - 1, column_y) for column_y in range(LY)]),
        "x_low": face_rows([(0, column_y) for column_y in range(LY)]),
        "y_high": face_rows([(column_x, LY - 1) for column_x in range(LX)]),
        "y_low": face_rows([(column_x, 0) for column_x in range(LX)]),
    }


def assemble_grid(interior, ghost_rows):
    channels = interior.shape[-1]
    top_len = (LY + 2) * LZ
    top_plane = ghost_rows[:top_len].reshape(1, LY + 2, LZ, channels)
    side_cols = ghost_rows[top_len : top_len + 2 * LX * LZ].reshape(LX, 2, LZ, channels)
    bottom_plane = ghost_rows[top_len + 2 * LX * LZ :].reshape(1, LY + 2, LZ, channels)
    middle = jnp.concatenate([side_cols[:, :1], interior, side_cols[:, 1:]], 1)
    return jnp.concatenate([top_plane, middle, bottom_plane], 0)


def frame_of(grid):
    channels = grid.shape[-1]
    side_cols = jnp.stack([grid[1:-1, 0], grid[1:-1, -1]], 1)
    return jnp.concatenate(
        [
            grid[0].reshape(-1, channels),
            side_cols.reshape(-1, channels),
            grid[-1].reshape(-1, channels),
        ],
        0,
    )


def shifted_columns(padded, start_x, start_y, span_x, span_y, starts_z):
    channels = padded.shape[-1]
    slab = padded[start_x : start_x + span_x, start_y : start_y + span_y]
    columns = jnp.concatenate([slab[:, :, start_z : start_z + LZ] for start_z in starts_z], -1)
    return columns.reshape(span_x * span_y * LZ, 3 * channels)


def return_along_y(piece, step):
    return shifted(piece, "gy", step)


def return_along_x(piece, step):
    return shifted(piece, "gx", step)


def local(features, w_sub, w_down, cell_ids, send_rows, map_in, map_out, cotangent):
    frames = frame_tables()
    row_count, channels = features.shape
    cell_count = LX * LY * LZ
    zero_row = jnp.zeros((1, channels), jnp.bfloat16)
    padded = jnp.concatenate([features, zero_row], 0)
    rim_rows = padded[send_rows]
    face_count = rim_rows.shape[0]
    plane_x = LY * LZ
    plane_y = (LX + 2) * LZ
    inner_y = LX * LZ
    beside_all = with_halo(rim_rows[None, None], (("gx", 0), ("gy", 1)), 1)
    flat_rows = beside_all.reshape(9 * face_count, channels)
    ghost_rows = flat_rows[
        jnp.asarray(frames["neighbour"] * face_count + frames["face"], jnp.int32)
    ]
    cell_slot = jnp.where(cell_ids >= 0, cell_ids, cell_count)
    dense_flat = (
        jnp.zeros((cell_count + 1, channels), jnp.bfloat16).at[cell_slot].set(features)[:cell_count]
    )
    active = jnp.zeros((cell_count + 1, 1), jnp.float32).at[cell_slot].set(1.0)[:cell_count]
    active = active.reshape(LX, LY, LZ, 1)
    grid = assemble_grid(dense_flat.reshape(LX, LY, LZ, channels), ghost_rows)
    grid = jnp.pad(grid, ((0, 0), (0, 0), (1, 1), (0, 0)))
    pre_act = jnp.zeros((cell_count, channels), jnp.float32)
    for step_x in range(3):
        for step_y in range(3):
            first = step_x * 9 + step_y * 3
            columns = shifted_columns(grid, step_x, step_y, LX, LY, (0, 1, 2))
            kernel = w_sub[first : first + 3].reshape(3 * channels, channels)
            pre_act = pre_act + jnp.dot(columns, kernel, preferred_element_type=jnp.float32)
    pre_act = pre_act.reshape(LX, LY, LZ, channels)
    hidden = (jax.nn.silu(pre_act) * active).astype(jnp.bfloat16)
    coarse_input = hidden.reshape(LX // 2, 2, LY // 2, 2, LZ // 2, 2, channels).transpose(
        0, 2, 4, 1, 3, 5, 6
    )
    coarse_input = coarse_input.reshape(U_DEV, 8 * channels)
    coarse = jnp.dot(coarse_input, w_down, preferred_element_type=jnp.float32).astype(jnp.bfloat16)
    back_rows = lax.dot_general(
        cotangent, w_down, (((1,), (1,)), ((), ())), preferred_element_type=jnp.float32
    ).astype(jnp.bfloat16)
    hidden_grad = back_rows.reshape(LX // 2, LY // 2, LZ // 2, 2, 2, 2, channels).transpose(
        0, 3, 1, 4, 2, 5, 6
    )
    hidden_grad = hidden_grad.reshape(LX, LY, LZ, channels)
    sigmoid_value = jax.nn.sigmoid(pre_act)
    pre_grad = (
        hidden_grad.astype(jnp.float32)
        * sigmoid_value
        * (1.0 + pre_act * (1.0 - sigmoid_value))
        * active
    ).astype(jnp.bfloat16)
    down_local = lax.dot_general(
        coarse_input, cotangent, (((0,), (0,)), ((), ())), preferred_element_type=jnp.float32
    )
    grad_flat = pre_grad.reshape(cell_count, channels)
    grad_padded = jnp.pad(pre_grad, ((2, 2), (2, 2), (1, 1), (0, 0)))
    weight_parts = []
    table_dense = jnp.zeros(((LX + 2) * (LY + 2) * LZ, channels), jnp.float32)
    for step_x in range(3):
        for step_y in range(3):
            first = step_x * 9 + step_y * 3
            columns = shifted_columns(grid, step_x, step_y, LX, LY, (0, 1, 2))
            part_grad = lax.dot_general(
                columns, grad_flat, (((0,), (0,)), ((), ())), preferred_element_type=jnp.float32
            )
            weight_parts.append(part_grad.reshape(3, channels, channels))
            back_columns = shifted_columns(
                grad_padded, 2 - step_x, 2 - step_y, LX + 2, LY + 2, (2, 1, 0)
            )
            flipped = jnp.swapaxes(w_sub[first : first + 3], 1, 2).reshape(3 * channels, channels)
            table_dense = table_dense + jnp.dot(
                back_columns, flipped, preferred_element_type=jnp.float32
            )
    sub_local = jnp.concatenate(weight_parts, 0)
    table_dense = table_dense.reshape(LX + 2, LY + 2, LZ, channels)
    sub_grad, down_grad = lax.psum((sub_local, down_local), ("gx", "gy"))
    ghost_grad = frame_of(table_dense)
    side_grad = ghost_grad[jnp.asarray(frames["side_order"], jnp.int32)]
    grad_west = side_grad[:plane_x]
    grad_east = side_grad[plane_x : 2 * plane_x]
    grad_south = side_grad[2 * plane_x : 2 * plane_x + plane_y]
    grad_north = side_grad[2 * plane_x + plane_y :]
    return_high = return_along_y(grad_south, -1)
    return_low = return_along_y(grad_north, 1)
    grad_west = (
        grad_west.at[(LY - 1) * LZ :]
        .add(return_high[inner_y : inner_y + LZ])
        .at[:LZ]
        .add(return_low[inner_y : inner_y + LZ])
    )
    grad_east = (
        grad_east.at[(LY - 1) * LZ :]
        .add(return_high[inner_y + LZ :])
        .at[:LZ]
        .add(return_low[inner_y + LZ :])
    )
    return_east = return_along_x(grad_west, -1)
    return_west = return_along_x(grad_east, 1)
    rim_grad = jnp.zeros((face_count, channels), jnp.float32)
    rim_grad = rim_grad.at[frames["x_high"]].add(return_east).at[frames["x_low"]].add(return_west)
    rim_grad = (
        rim_grad.at[frames["y_high"]]
        .add(return_high[:inner_y])
        .at[frames["y_low"]]
        .add(return_low[:inner_y])
    )
    interior_grad = table_dense[1:-1, 1:-1].reshape(cell_count, channels)
    interior_grad = jnp.concatenate([interior_grad, jnp.zeros((1, channels), jnp.float32)], 0)
    own_grad = interior_grad[cell_slot]
    own_grad = (
        jnp.concatenate([own_grad, jnp.zeros((1, channels), jnp.float32)], 0)
        .at[send_rows]
        .add(rim_grad)[:row_count]
    )
    feature_grad = own_grad.astype(jnp.bfloat16)
    return (coarse, feature_grad, sub_grad, down_grad)


def solution(mesh):
    placed = (
        P(("gx", "gy"), None),
        P(),
        P(),
        P(("gx", "gy")),
        P(("gx", "gy")),
        P(None, ("gx", "gy")),
        P(None, ("gx", "gy")),
        P(("gx", "gy"), None),
    )
    return jax.shard_map(
        local,
        mesh=mesh,
        in_specs=placed,
        out_specs=(P(("gx", "gy"), None), P(("gx", "gy"), None), P(), P()),
        check_vma=False,
    )
```

profile of v0, /device:TPU:2, one launch (start us, length us, event | category | flops | bytes accessed | tf_op | source)
XLA Modules:
  0.0 361.6 jit_solution(8910161390339559812)
XLA Ops:
  7.2 0.7 compare_select_fusion
  8.0 0.5 copy-done.55
  8.5 0.8 concatenate.119
  9.3 1.4 gather_fusion
  10.7 1.9 collective-permute-start.1
  12.6 2.4 collective-permute-start
  15.1 2.4 slice_bitcast_fusion.2
  17.7 1.4 scatter_custom_fusion.1
  19.2 0.7 mul.58
  20.1 1.5 scatter_custom_fusion
  21.6 0.9 copy.96
  22.7 0.8 copy.98
  23.7 0.8 copy.99
  24.4 0.7 copy.100
  25.2 0.7 copy.101
  25.9 0.8 copy.102
  26.7 0.7 copy.103
  27.4 0.7 copy.104
  28.2 0.7 copy.105
  28.9 0.7 copy.106
  29.7 1.3 collective-permute-start.3
  31.0 6.2 %collective-permute-start.2 = (bf16[3,1,288,128]{3,2,1,0:T(8,128)(2,1)S(1)}, bf16[3,1,288,128]{3,2,1,0:T(8,128)(2,1)S(1)}, u32[]{:S(2)}, u32[]{:S(2)}) collective-permute-start(bf16[3,1,288,128]{3,2,1,0:T(8,128)(2,1)S(1)} %pad_maximum_fusion.19), channel_id=1, source_target_pairs={{0,1},{1,2},{2,3},{3,4},{4,5},{5,6},{6,7},{7,8},{8,9},{9,10},{10,1... | collective-permute-start | bytes 663560 | tf_op jit(solution)/shard_map/ppermute | solution.py:24
  37.3 0.6 pad_clamp_fusion
  37.9 2.5 collective-permute-done.3
  40.4 4.7 %collective-permute-done.2 = bf16[3,1,288,128]{3,2,1,0:T(8,128)(2,1)S(1)} collective-permute-done((bf16[3,1,288,128]{3,2,1,0:T(8,128)(2,1)S(1)}, bf16[3,1,288,128]{3,2,1,0:T(8,128)(2,1)S(1)}, u32[]{:S(2)}, u32[]{:S(2)}) %collective-permute-start.2) | collective-permute-done | bytes 221216 | tf_op jit(solution)/shard_map/ppermute | solution.py:24
  45.2 1.4 gather_fusion.1
  47.5 0.8 fusion.11
  50.4 0.6 copy-done.51
  51.9 0.7 copy-done.13
  52.8 1.3 pad_slice_fusion.1
  54.1 2.3 pad_slice_fusion.2
  56.4 1.9 copy.116
  58.3 2.0 copy.112
  60.2 0.9 copy.115
  61.4 0.9 copy.110
  62.3 0.9 copy.109
  63.3 0.9 fusion.21
  64.4 0.9 copy.108
  65.3 0.9 copy.111
  66.2 1.0 copy.113
  67.2 1.3 fusion.47
  70.0 0.6 copy-done.30
  71.1 0.6 copy-done.48
  75.0 0.5 copy-done.15
  76.2 0.4 copy-done.43
  77.7 0.6 copy-done.10
  80.8 1.2 copy-done.1
  82.1 1.1 gather_fusion.3
  83.2 1.3 collective-permute-start.4
  84.5 6.5 %collective-permute-start.5 = (f32[48,128]{1,0:T(8,128)S(1)}, f32[48,128]{1,0:T(8,128)S(1)}, u32[]{:S(2)}, u32[]{:S(2)}) collective-permute-start(f32[48,128]{1,0:T(8,128)S(1)} %get-tuple-element.104), channel_id=1, source_target_pairs={{0,1},{1,2},{2,3},{3,4},{4,5},{5,6},{6,7},{7,8},{8,9},{9,10},{10,1... | collective-permute-start | bytes 73736 | tf_op jit(solution)/shard_map/ppermute | solution.py:16
  91.1 1.5 collective-permute-done.5
  92.5 1.9 collective-permute-start.7
  94.5 3.6 %collective-permute-start.6 = (f32[128,128]{1,0:T(8,128)S(1)}, f32[128,128]{1,0:T(8,128)S(1)}, u32[]{:S(2)}, u32[]{:S(2)}) collective-permute-start(f32[128,128]{1,0:T(8,128)S(1)} %get-tuple-element.140), channel_id=1, source_target_pairs={{16,0},{32,16},{48,32},{64,48},{80,64},{96,80},{112,96},{128,112},... | collective-permute-start | bytes 196616 | tf_op jit(solution)/shard_map/ppermute | solution.py:16
  98.1 0.8 convolution_convert_fusion.1
  99.0 0.9 gather_fusion.2
  100.0 1.1 scatter_custom_fusion.2
  101.2 1.3 scatter_fusion
  102.5 0.9 scatter_custom_fusion.4
  103.4 0.9 scatter_custom_fusion.5
  104.3 2.1 scatter_fusion.1
  106.5 0.6 slice.681
  107.1 243.8 %all-reduce.8.cloned.1.call-done = (f32[27,128,128]{2,1,0:T(8,128)}, f32[1024,256]{1,0:T(8,128)}) async-done(((f32[27,128,128]{2,1,0:T(8,128)}, f32[1024,256]{1,0:T(8,128)}), (f32[27,128,128]{2,1,0:T(8,128)}, f32[1024,256]{1,0:T(8,128)})) %all-reduce.8.cloned.1.call-update) | async-done | bytes 2818064 | tf_op jit(solution)/shard_map/psum | solution.py:190
  350.8 3.0 copy.138
  353.8 1.0 copy.139
  (196 shorter events, 14.7 us)
Async XLA Ops:
  7.2 10.3 %copy-start = (bf16[1024,256]{1,0:T(8,128)(2,1)S(1)}, bf16[1024,256]{1,0:T(8,128)(2,1)}, u32[]{:S(2)}) copy-start(bf16[1024,256]{1,0:T(8,128)(2,1)} %param.28) | copy-start | bytes 1572868
  7.2 343.7 %all-reduce.8.cloned.1.call-start = ((), (), s32[]{:S(2)}) async-start(), calls=%async_computation | async-start | bytes 5636096 | tf_op jit(solution)/shard_map/psum | solution.py:190
  10.7 6.7 %copy-start.52 = (bf16[64,256]{1,0:T(8,128)(2,1)S(1)}, bf16[64,256]{1,0:T(8,128)(2,1)}, u32[]{:S(2)}) copy-start(bf16[64,256]{1,0:T(8,128)(2,1)} %param.31) | copy-start | bytes 98308
  10.7 7.0 %copy-start.60 = (s32[256]{0:T(256)S(1)}, s32[256]{0:T(256)}, u32[]{:S(2)}) copy-start(s32[256]{0:T(256)} %param.29) | copy-start | bytes 3076
  10.7 19.0 %collective-permute-start.1 = (bf16[1,1,288,128]{3,2,1,0:T(8,128)(2,1)S(1)}, bf16[1,1,288,128]{3,2,1,0:T(8,128)(2,1)S(1)}, u32[]{:S(2)}, u32[]{:S(2)}) collective-permute-start(bf16[1,1,288,128]{3,2,1,0:T(8,128)(2,1)S(1)} %bitcast.218), channel_id=1, source_target_pairs={{16,0},{32,16},{48,32},{64,48},{80,64},{96,80},{112,96},{128,112},... | collective-permute-start | bytes 221192 | tf_op jit(solution)/shard_map/ppermute | solution.py:27
  12.6 17.0 %collective-permute-start = (bf16[1,1,288,128]{3,2,1,0:T(8,128)(2,1)S(1)}, bf16[1,1,288,128]{3,2,1,0:T(8,128)(2,1)S(1)}, u32[]{:S(2)}, u32[]{:S(2)}) collective-permute-start(bf16[1,1,288,128]{3,2,1,0:T(8,128)(2,1)S(1)} %bitcast.219), channel_id=1, source_target_pairs={{0,16},{16,32},{32,48},{48,64},{64,80},{80,96},{96,112},{112,128},... | collective-permute-start | bytes 221192 | tf_op jit(solution)/shard_map/ppermute | solution.py:24
  22.7 14.6 %copy-start.58 = (s32[352]{0:T(512)S(1)}, s32[352]{0:T(512)}, u32[]{:S(2)}) copy-start(s32[352]{0:T(512)} %constant.171) | copy-start | bytes 4228
  22.7 14.6 %copy-start.59 = (s32[352]{0:T(512)S(1)}, s32[352]{0:T(512)}, u32[]{:S(2)}) copy-start(s32[352]{0:T(512)} %constant.173) | copy-start | bytes 4228
  29.7 10.7 %collective-permute-start.3 = (bf16[3,1,288,128]{3,2,1,0:T(8,128)(2,1)S(1)}, bf16[3,1,288,128]{3,2,1,0:T(8,128)(2,1)S(1)}, u32[]{:S(2)}, u32[]{:S(2)}) collective-permute-start(bf16[3,1,288,128]{3,2,1,0:T(8,128)(2,1)S(1)} %pad_maximum_fusion.19), channel_id=1, source_target_pairs={{1,0},{2,1},{3,2},{4,3},{5,4},{6,5},{7,6},{8,7},{9,8},{10,9},{11,1... | collective-permute-start | bytes 663560 | tf_op jit(solution)/shard_map/ppermute | solution.py:27
  31.0 14.1 %collective-permute-start.2 = (bf16[3,1,288,128]{3,2,1,0:T(8,128)(2,1)S(1)}, bf16[3,1,288,128]{3,2,1,0:T(8,128)(2,1)S(1)}, u32[]{:S(2)}, u32[]{:S(2)}) collective-permute-start(bf16[3,1,288,128]{3,2,1,0:T(8,128)(2,1)S(1)} %pad_maximum_fusion.19), channel_id=1, source_target_pairs={{0,1},{1,2},{2,3},{3,4},{4,5},{5,6},{6,7},{7,8},{8,9},{9,10},{10,1... | collective-permute-start | bytes 663560 | tf_op jit(solution)/shard_map/ppermute | solution.py:24
  50.0 1.6 copy-start.2
  50.0 1.0 copy-start.51
  50.3 1.0 copy-start.50
  50.4 1.2 copy-start.12
  50.4 1.2 copy-start.54
  51.3 1.4 copy-start.53
  61.4 1.9 copy-start.14
  65.3 3.2 copy-start.32
  65.3 3.2 copy-start.33
  65.3 3.2 copy-start.41
  67.2 1.5 copy-start.49
  68.5 1.0 copy-start.39
  68.5 1.1 copy-start.40
  68.6 1.2 copy-start.31
  68.6 1.2 copy-start.36
  68.6 1.3 copy-start.37
  69.6 1.0 copy-start.30
  69.6 1.0 copy-start.34
  69.7 1.1 copy-start.35
  69.9 1.0 copy-start.27
  69.9 1.0 copy-start.28
  69.9 1.1 copy-start.29
  71.0 1.0 copy-start.24
  71.1 1.0 copy-start.25
  71.1 1.2 copy-start.26
  71.7 1.0 copy-start.47
  72.2 0.9 copy-start.21
  72.2 1.0 copy-start.22
  72.2 1.2 copy-start.23
  72.7 1.0 copy-start.46
  73.4 0.9 copy-start.18
  73.4 1.0 copy-start.19
  73.4 1.2 copy-start.20
  73.6 1.0 copy-start.45
  74.5 1.0 copy-start.16
  74.5 1.2 copy-start.17
  74.6 1.2 copy-start.44
  75.8 1.1 copy-start.42
  77.3 1.0 copy-start.10
  77.3 1.3 copy-start.7
  77.3 1.5 copy-start.6
  77.7 1.5 copy-start.9
  78.3 1.1 copy-start.5
  78.6 1.1 copy-start.8
  79.1 1.1 copy-start.4
  79.4 1.1 copy-start.3
  80.8 1.2 copy-start.1
  80.8 1.3 copy-start.57
  83.2 7.8 %collective-permute-start.4 = (f32[48,128]{1,0:T(8,128)S(1)}, f32[48,128]{1,0:T(8,128)S(1)}, u32[]{:S(2)}, u32[]{:S(2)}) collective-permute-start(f32[48,128]{1,0:T(8,128)S(1)} %get-tuple-element.105), channel_id=1, source_target_pairs={{1,0},{2,1},{3,2},{4,3},{5,4},{6,5},{7,6},{8,7},{9,8},{10,9},{11,1... | collective-permute-start | bytes 73736 | tf_op jit(solution)/shard_map/ppermute | solution.py:16
  84.5 8.0 %collective-permute-start.5 = (f32[48,128]{1,0:T(8,128)S(1)}, f32[48,128]{1,0:T(8,128)S(1)}, u32[]{:S(2)}, u32[]{:S(2)}) collective-permute-start(f32[48,128]{1,0:T(8,128)S(1)} %get-tuple-element.104), channel_id=1, source_target_pairs={{0,1},{1,2},{2,3},{3,4},{4,5},{5,6},{6,7},{7,8},{8,9},{9,10},{10,1... | collective-permute-start | bytes 73736 | tf_op jit(solution)/shard_map/ppermute | solution.py:16
  92.5 8.6 %collective-permute-start.7 = (f32[128,128]{1,0:T(8,128)S(1)}, f32[128,128]{1,0:T(8,128)S(1)}, u32[]{:S(2)}, u32[]{:S(2)}) collective-permute-start(f32[128,128]{1,0:T(8,128)S(1)} %get-tuple-element.139), channel_id=1, source_target_pairs={{0,16},{16,32},{32,48},{48,64},{64,80},{80,96},{96,112},{112,128},... | collective-permute-start | bytes 196616 | tf_op jit(solution)/shard_map/ppermute | solution.py:16
  94.5 5.5 %collective-permute-start.6 = (f32[128,128]{1,0:T(8,128)S(1)}, f32[128,128]{1,0:T(8,128)S(1)}, u32[]{:S(2)}, u32[]{:S(2)}) collective-permute-start(f32[128,128]{1,0:T(8,128)S(1)} %get-tuple-element.140), channel_id=1, source_target_pairs={{16,0},{32,16},{48,32},{64,48},{80,64},{96,80},{112,96},{128,112},... | collective-permute-start | bytes 196616 | tf_op jit(solution)/shard_map/ppermute | solution.py:16
  99.0 5.3 %copy-start.56 = (s32[288]{0:T(512)S(1)}, s32[288]{0:T(512)}, u32[]{:S(2)}) copy-start(s32[288]{0:T(512)} %copy-done.55) | copy-start | bytes 3460
  350.8 3.0 copy-start.11
  (6 other events, 4.9 us)
Sparse Core Ops, SparseCore 0:
  82.1 268.6 all-reduce.7
where the time goes:
time: 363 us; the launch traced here: 362 us
  waiting for transfers between devices  253 us (70%)
  local copies, waits for them, and re-layouts  47.3 us (13%)
  starting transfers between devices  25.3 us (7%)
  between operations  15.1 us (4%)
  other arithmetic  11.2 us (3%)
  matrix products  10.2 us (3%)
    psum x1, waiting for transfers between devices, local(): sub_grad, down_grad = lax.psum((sub_local, down_local), ('gx', 'gy'))  244 us
    ppermute x4, starting transfers between devices, shifted(): return lax.ppermute(value, axis, pairs)  13.4 us
    unnamed x124, local copies, waits for them, and re-layouts  12.7 us
    dot_general x9, local copies, waits for them, and re-layouts, local(): lax.dot_general(columns, grad_flat, (((0,), (0,)), ((), ())), preferred_e...  9.73 us
    ppermute x2, starting transfers between devices, with_halo(): lax.ppermute(lax.slice_in_dim(block, block.shape[dim] - width, None, axis...  8.65 us
    transpose x10, local copies, waits for them, and re-layouts, local(): jnp.swapaxes(w_sub[first:first + 3], 1, 2).reshape(3 * channels, channels)  8.48 us
  transfers between devices with their start and end apart: 9, of which 5 were waited for; matrix products, arithmetic and copies ran while one was open for 7% of the time, Pallas kernels for 0%

commit v1 on v0

--- a/solution.py
+++ b/solution.py
@@ -8,6 +8,11 @@
 LY = 16
 LZ = 8
 U_DEV = 64
+
+
+def one_after_other(value_2, leading, second):
+    inner = lax.psum(value_2, leading)
+    return lax.psum(inner, second)
 
 
 def shifted(value, axis, by):
@@ -187,7 +192,7 @@
             )
     sub_local = jnp.concatenate(weight_parts, 0)
     table_dense = table_dense.reshape(LX + 2, LY + 2, LZ, channels)
-    sub_grad, down_grad = lax.psum((sub_local, down_local), ("gx", "gy"))
+    sub_grad, down_grad = one_after_other((sub_local, down_local), "gx", "gy")
     ghost_grad = frame_of(table_dense)
     side_grad = ghost_grad[jnp.asarray(frames["side_order"], jnp.int32)]
     grad_west = side_grad[:plane_x]

time: 363 us -> 400 us (1.10)
  waiting for transfers between devices: 253 us -> 293 us
  local copies, waits for them, and re-layouts: 47.3 us -> 42.3 us
    psum x1 -> x2, waiting for transfers between devices: 244 us -> 284 us  [the longest x1 154 us: one_after_other(): return lax.psum(inner, second)]
    unnamed x124 -> x114, local copies, waits for them, and re-layouts: 12.7 us -> 9.86 us
  transfers between devices with their start and end apart: 9 -> 10, of which waited for: 5 -> 6; matrix products, arithmetic and copies ran while one was open for 7% -> 8% of each run, Pallas kernels for 0% -> 0%
where the time goes in v1:
time: 400 us; the launch traced here: 398 us
  waiting for transfers between devices  293 us (73%)
  local copies, waits for them, and re-layouts  42.3 us (11%)
  starting transfers between devices  24.8 us (6%)
  between operations  15.2 us (4%)
  matrix products  11.2 us (3%)
  other arithmetic  11 us (3%)
    psum x1, waiting for transfers between devices, one_after_other(): return lax.psum(inner, second)  154 us
    psum x1, waiting for transfers between devices, one_after_other(): inner = lax.psum(value_2, leading)  130 us
    ppermute x4, starting transfers between devices, shifted(): return lax.ppermute(value, axis, pairs)  12.9 us
    unnamed x114, local copies, waits for them, and re-layouts  9.86 us
    transpose x10, local copies, waits for them, and re-layouts, local(): jnp.swapaxes(w_sub[first:first + 3], 1, 2).reshape(3 * channels, channels)  8.99 us
    ppermute x2, starting transfers between devices, with_halo(): lax.ppermute(lax.slice_in_dim(block, block.shape[dim] - width, None, axis...  8.47 us
  transfers between devices with their start and end apart: 10, of which 6 were waited for; matrix products, arithmetic and copies ran while one was open for 8% of the time, Pallas kernels for 0%

profile of v1, /device:TPU:2, one launch (start us, length us, event | category | flops | bytes accessed | tf_op | source)
XLA Modules:
  0.0 397.7 jit_solution(7517634926223583169)
XLA Ops:
  7.2 0.7 compare_select_fusion
  8.0 0.6 copy-done.50
  8.5 0.8 concatenate.119
  9.4 1.4 gather_fusion
  10.8 1.9 collective-permute-start.1
  12.7 2.4 collective-permute-start
  15.1 2.3 slice_bitcast_fusion.2
  17.8 1.4 scatter_custom_fusion.1
  19.2 0.7 mul.58
  20.1 1.5 scatter_custom_fusion
  21.6 0.9 copy.96
  22.8 0.8 copy.98
  23.6 0.7 copy.107
  24.3 0.7 copy.99
  25.1 0.7 copy.100
  25.8 0.7 copy.101
  26.6 0.7 copy.102
  27.3 0.7 copy.103
  28.1 0.7 copy.104
  28.8 0.7 copy.105
  29.5 0.7 copy.106
  30.3 1.3 collective-permute-start.3
  31.6 6.1 %collective-permute-start.2 = (bf16[3,1,288,128]{3,2,1,0:T(8,128)(2,1)S(1)}, bf16[3,1,288,128]{3,2,1,0:T(8,128)(2,1)S(1)}, u32[]{:S(2)}, u32[]{:S(2)}) collective-permute-start(bf16[3,1,288,128]{3,2,1,0:T(8,128)(2,1)S(1)} %pad_maximum_fusion.19), channel_id=1, source_target_pairs={{0,1},{1,2},{2,3},{3,4},{4,5},{5,6},{6,7},{7,8},{8,9},{9,10},{10,1... | collective-permute-start | bytes 663560 | tf_op jit(solution)/shard_map/ppermute | solution.py:29
  37.7 0.6 pad_clamp_fusion
  38.3 2.7 collective-permute-done.3
  41.0 4.7 %collective-permute-done.2 = bf16[3,1,288,128]{3,2,1,0:T(8,128)(2,1)S(1)} collective-permute-done((bf16[3,1,288,128]{3,2,1,0:T(8,128)(2,1)S(1)}, bf16[3,1,288,128]{3,2,1,0:T(8,128)(2,1)S(1)}, u32[]{:S(2)}, u32[]{:S(2)}) %collective-permute-start.2) | collective-permute-done | bytes 221216 | tf_op jit(solution)/shard_map/ppermute | solution.py:29
  45.8 1.4 gather_fusion.1
  47.6 0.8 fusion.41
  48.5 1.0 fusion.39
  49.5 1.0 copy.116
  50.5 1.0 copy.112
  51.6 0.9 copy.115
  52.6 0.9 copy.114
  53.6 1.0 copy.110
  54.6 0.9 copy.109
  55.5 1.4 fusion.8
  60.8 0.9 copy.108
  61.8 0.9 copy.111
  62.9 1.3 fusion.47
  64.2 1.3 convolution_dynamic-update-slice_fusion.8
  67.8 1.2 copy-done.1
  69.4 1.0 pad_slice_fusion.1
  70.6 0.6 pad_slice_fusion.2
  71.7 0.7 copy-done.34
  74.9 129.8 %all-reduce.12.cloned.1.call-done = (f32[27,128,128]{2,1,0:T(8,128)}, f32[1024,256]{1,0:T(8,128)}) async-done(((f32[27,128,128]{2,1,0:T(8,128)}, f32[1024,256]{1,0:T(8,128)}), (f32[27,128,128]{2,1,0:T(8,128)}, f32[1024,256]{1,0:T(8,128)})) %all-reduce.12.cloned.1.call-update) | async-done | bytes 2818064 | tf_op jit(solution)/shard_map/psum | solution.py:14
  204.8 0.9 copy-done.18
  206.1 0.6 copy-done.28
  208.1 1.1 gather_fusion.3
  209.2 1.3 collective-permute-start.4
  210.5 6.1 %collective-permute-start.5 = (f32[48,128]{1,0:T(8,128)S(1)}, f32[48,128]{1,0:T(8,128)S(1)}, u32[]{:S(2)}, u32[]{:S(2)}) collective-permute-start(f32[48,128]{1,0:T(8,128)S(1)} %get-tuple-element.106), channel_id=1, source_target_pairs={{0,1},{1,2},{2,3},{3,4},{4,5},{5,6},{6,7},{7,8},{8,9},{9,10},{10,1... | collective-permute-start | bytes 73736 | tf_op jit(solution)/shard_map/ppermute | solution.py:21
  216.6 1.5 collective-permute-done.5
  218.1 1.9 collective-permute-start.7
  220.0 3.6 collective-permute-start.6
  223.7 0.8 convolution_convert_fusion.1
  224.5 0.9 gather_fusion.2
  225.6 1.1 scatter_custom_fusion.2
  226.7 1.3 scatter_fusion
  228.0 0.9 scatter_custom_fusion.4
  229.0 0.9 scatter_custom_fusion.5
  229.9 2.1 scatter_fusion.1
  232.0 0.6 slice.681
  232.6 154.3 %all-reduce.10.cloned.1.call-done = (f32[27,128,128]{2,1,0:T(8,128)}, f32[1024,256]{1,0:T(8,128)}) async-done(((f32[27,128,128]{2,1,0:T(8,128)}, f32[1024,256]{1,0:T(8,128)}), (f32[27,128,128]{2,1,0:T(8,128)}, f32[1024,256]{1,0:T(8,128)})) %all-reduce.10.cloned.1.call-update) | async-done | bytes 2818064 | tf_op jit(solution)/shard_map/psum | solution.py:15
  386.9 3.0 copy.140
  389.9 1.0 copy.141
  (189 shorter events, 13.0 us)
Async XLA Ops:
  7.2 10.3 %copy-start = (bf16[1024,256]{1,0:T(8,128)(2,1)S(1)}, bf16[1024,256]{1,0:T(8,128)(2,1)}, u32[]{:S(2)}) copy-start(bf16[1024,256]{1,0:T(8,128)(2,1)} %param.28) | copy-start | bytes 1572868
  7.2 197.5 %all-reduce.12.cloned.1.call-start = ((), (), s32[]{:S(2)}) async-start(), calls=%async_computation.1 | async-start | bytes 5636096 | tf_op jit(solution)/shard_map/psum | solution.py:14
  10.8 6.7 %copy-start.42 = (bf16[64,256]{1,0:T(8,128)(2,1)S(1)}, bf16[64,256]{1,0:T(8,128)(2,1)}, u32[]{:S(2)}) copy-start(bf16[64,256]{1,0:T(8,128)(2,1)} %param.31) | copy-start | bytes 98308
  10.8 6.9 %copy-start.55 = (s32[256]{0:T(256)S(1)}, s32[256]{0:T(256)}, u32[]{:S(2)}) copy-start(s32[256]{0:T(256)} %param.29) | copy-start | bytes 3076
  10.8 19.5 %collective-permute-start.1 = (bf16[1,1,288,128]{3,2,1,0:T(8,128)(2,1)S(1)}, bf16[1,1,288,128]{3,2,1,0:T(8,128)(2,1)S(1)}, u32[]{:S(2)}, u32[]{:S(2)}) collective-permute-start(bf16[1,1,288,128]{3,2,1,0:T(8,128)(2,1)S(1)} %bitcast.218), channel_id=1, source_target_pairs={{16,0},{32,16},{48,32},{64,48},{80,64},{96,80},{112,96},{128,112},... | collective-permute-start | bytes 221192 | tf_op jit(solution)/shard_map/ppermute | solution.py:32
  12.7 17.6 %collective-permute-start = (bf16[1,1,288,128]{3,2,1,0:T(8,128)(2,1)S(1)}, bf16[1,1,288,128]{3,2,1,0:T(8,128)(2,1)S(1)}, u32[]{:S(2)}, u32[]{:S(2)}) collective-permute-start(bf16[1,1,288,128]{3,2,1,0:T(8,128)(2,1)S(1)} %bitcast.219), channel_id=1, source_target_pairs={{0,16},{16,32},{32,48},{48,64},{64,80},{80,96},{96,112},{112,128},... | collective-permute-start | bytes 221192 | tf_op jit(solution)/shard_map/ppermute | solution.py:29
  19.2 0.7 copy-start.48
  22.7 15.0 %copy-start.53 = (s32[352]{0:T(512)S(1)}, s32[352]{0:T(512)}, u32[]{:S(2)}) copy-start(s32[352]{0:T(512)} %constant.171) | copy-start | bytes 4228
  22.7 15.0 %copy-start.54 = (s32[352]{0:T(512)S(1)}, s32[352]{0:T(512)}, u32[]{:S(2)}) copy-start(s32[352]{0:T(512)} %constant.173) | copy-start | bytes 4228
  30.3 10.7 %collective-permute-start.3 = (bf16[3,1,288,128]{3,2,1,0:T(8,128)(2,1)S(1)}, bf16[3,1,288,128]{3,2,1,0:T(8,128)(2,1)S(1)}, u32[]{:S(2)}, u32[]{:S(2)}) collective-permute-start(bf16[3,1,288,128]{3,2,1,0:T(8,128)(2,1)S(1)} %pad_maximum_fusion.19), channel_id=1, source_target_pairs={{1,0},{2,1},{3,2},{4,3},{5,4},{6,5},{7,6},{8,7},{9,8},{10,9},{11,1... | collective-permute-start | bytes 663560 | tf_op jit(solution)/shard_map/ppermute | solution.py:32
  31.6 14.1 %collective-permute-start.2 = (bf16[3,1,288,128]{3,2,1,0:T(8,128)(2,1)S(1)}, bf16[3,1,288,128]{3,2,1,0:T(8,128)(2,1)S(1)}, u32[]{:S(2)}, u32[]{:S(2)}) collective-permute-start(bf16[3,1,288,128]{3,2,1,0:T(8,128)(2,1)S(1)} %pad_maximum_fusion.19), channel_id=1, source_target_pairs={{0,1},{1,2},{2,3},{3,4},{4,5},{5,6},{6,7},{7,8},{8,9},{9,10},{10,1... | collective-permute-start | bytes 663560 | tf_op jit(solution)/shard_map/ppermute | solution.py:29
  49.4 2.0 copy-start.20
  49.4 2.0 copy-start.22
  49.5 2.0 copy-start.2
  51.5 2.0 copy-start.24
  51.6 1.9 copy-start.25
  55.5 1.4 copy-start.35
  55.5 1.7 copy-start.41
  56.9 0.9 copy-start.40
  56.9 1.2 copy-start.39
  57.2 1.2 copy-start.21
  57.2 1.2 copy-start.23
  57.2 1.2 copy-start.47
  58.1 0.9 copy-start.38
  58.4 0.9 copy-start.37
  58.7 0.9 copy-start.36
  59.0 1.0 copy-start.3
  59.0 1.1 copy-start.12
  59.0 1.1 copy-start.46
  59.0 1.1 copy-start.49
  59.6 0.9 copy-start.44
  60.5 2.5 copy-start.14
  60.7 2.2 copy-start.43
  62.7 2.9 copy-start.9
  62.9 2.9 copy-start.8
  64.2 1.9 copy-start.10
  64.2 2.2 copy-start.5
  65.8 1.1 copy-start.7
  66.1 1.1 copy-start.6
  66.4 1.1 copy-start.4
  67.8 1.2 copy-start.1
  67.8 1.5 copy-start.13
  67.8 1.5 copy-start.15
  67.8 1.5 copy-start.45
  69.0 317.9 %all-reduce.10.cloned.1.call-start = ((), (), s32[]{:S(2)}) async-start(), calls=%async_computation | async-start | bytes 5636096 | tf_op jit(solution)/shard_map/psum | solution.py:15
  71.5 0.9 copy-start.34
  71.6 1.1 copy-start.33
  72.4 0.9 copy-start.32
  72.7 0.9 copy-start.31
  73.3 0.9 copy-start.30
  73.7 0.9 copy-start.29
  204.7 0.9 copy-start.18
  204.7 1.0 copy-start.19
  204.7 1.1 copy-start.16
  204.8 1.2 copy-start.17
  205.8 0.9 copy-start.28
  206.0 1.0 copy-start.27
  206.7 0.9 copy-start.26
  209.2 7.4 %collective-permute-start.4 = (f32[48,128]{1,0:T(8,128)S(1)}, f32[48,128]{1,0:T(8,128)S(1)}, u32[]{:S(2)}, u32[]{:S(2)}) collective-permute-start(f32[48,128]{1,0:T(8,128)S(1)} %get-tuple-element.107), channel_id=1, source_target_pairs={{1,0},{2,1},{3,2},{4,3},{5,4},{6,5},{7,6},{8,7},{9,8},{10,9},{11,1... | collective-permute-start | bytes 73736 | tf_op jit(solution)/shard_map/ppermute | solution.py:21
  210.5 7.6 %collective-permute-start.5 = (f32[48,128]{1,0:T(8,128)S(1)}, f32[48,128]{1,0:T(8,128)S(1)}, u32[]{:S(2)}, u32[]{:S(2)}) collective-permute-start(f32[48,128]{1,0:T(8,128)S(1)} %get-tuple-element.106), channel_id=1, source_target_pairs={{0,1},{1,2},{2,3},{3,4},{4,5},{5,6},{6,7},{7,8},{8,9},{9,10},{10,1... | collective-permute-start | bytes 73736 | tf_op jit(solution)/shard_map/ppermute | solution.py:21
  218.1 8.6 %collective-permute-start.7 = (f32[128,128]{1,0:T(8,128)S(1)}, f32[128,128]{1,0:T(8,128)S(1)}, u32[]{:S(2)}, u32[]{:S(2)}) collective-permute-start(f32[128,128]{1,0:T(8,128)S(1)} %get-tuple-element.141), channel_id=1, source_target_pairs={{0,16},{16,32},{32,48},{48,64},{64,80},{80,96},{96,112},{112,128},... | collective-permute-start | bytes 196616 | tf_op jit(solution)/shard_map/ppermute | solution.py:21
  220.0 5.5 %collective-permute-start.6 = (f32[128,128]{1,0:T(8,128)S(1)}, f32[128,128]{1,0:T(8,128)S(1)}, u32[]{:S(2)}, u32[]{:S(2)}) collective-permute-start(f32[128,128]{1,0:T(8,128)S(1)} %get-tuple-element.142), channel_id=1, source_target_pairs={{16,0},{32,16},{48,32},{64,48},{80,64},{96,80},{112,96},{128,112},... | collective-permute-start | bytes 196616 | tf_op jit(solution)/shard_map/ppermute | solution.py:21
  224.5 5.3 %copy-start.51 = (s32[288]{0:T(512)S(1)}, s32[288]{0:T(512)}, u32[]{:S(2)}) copy-start(s32[288]{0:T(512)} %copy-done.50) | copy-start | bytes 3460
  386.9 3.0 copy-start.11
  (2 other events, 1.3 us)
Sparse Core Ops, SparseCore 0:
  69.1 135.5 all-reduce.11
  207.5 179.4 all-reduce.9
